TPU v7x, 32 devices: a whole 2x2x4 slice. The times are simulated.
32 devices in a mesh: groups: 2 (over y), row: 4 (over z), col: 2 (over x), rep: 2 (over core).
Axes of the slice: x: 2, y: 2, z: 4, core: 2. Of those that a mesh axis runs over, the one named last changes fastest.
Arguments:
- latents: bfloat16 [2048, 128], P(('groups', 'row', 'col', 'rep')), parts along dimension 0, may hold values from -6 to 6
- saved_sum: bfloat16 [2048, 128], P(('groups', 'row', 'col', 'rep')), parts along dimension 0, may hold values from -12 to 12
- grad_latents_out: bfloat16 [2048, 128], P(('groups', 'row', 'col', 'rep')), parts along dimension 0, may hold values from -6 to 6
- edge_latents: bfloat16 [1024, 128, 128], P(('groups', 'row', 'col', 'rep')), parts along dimension 0, may hold values from -6 to 6
- grad_edges_out: bfloat16 [1024, 128, 128], P(('groups', 'row', 'col', 'rep')), parts along dimension 0, may hold values from -6 to 6
- recv_slot: int32 [1024, 128], P(('groups', 'row', 'col', 'rep')), parts along dimension 0, may hold values from -1 to 127
- send_slot: int32 [1024, 128], P(('groups', 'row', 'col', 'rep')), parts along dimension 0, may hold values from 0 to 127
- tile_recv: int32 [1024], P(('groups', 'row', 'col', 'rep')), parts along dimension 0, may hold values from 0 to 3
- tile_send: int32 [1024], P(('groups', 'row', 'col', 'rep')), parts along dimension 0, may hold values from 0 to 1
- tile_count: int32 [32], P(('groups', 'row', 'col', 'rep')), parts along dimension 0, may hold values from 4 to 32, as said below
- edge_first: bfloat16 [384, 128], replicated, may hold values from -0.3125 to 0.3125
- edge_second: bfloat16 [128, 128], replicated, may hold values from -0.5 to 0.5
- edge_gain: float32 [128], replicated, may hold values from 0.5 to 1.5
- node_first: bfloat16 [256, 128], replicated, may hold values from -0.375 to 0.375
- node_second: bfloat16 [128, 128], replicated, may hold values from -0.5 to 0.5
- node_gain: float32 [128], replicated, may hold values from 0.5 to 1.5
Outputs:
- grad_latents: bfloat16 [2048, 128], P(('groups', 'row', 'col', 'rep')), parts along dimension 0
- grad_edges: bfloat16 [1024, 128, 128], P(('groups', 'row', 'col', 'rep')), parts along dimension 0
- grad_edge_first: float32 [768, 128], P('groups'), parts along dimension 0
- grad_edge_second: float32 [256, 128], P('groups'), parts along dimension 0
- grad_edge_gain: float32 [256], P('groups'), parts along dimension 0
- grad_node_first: float32 [512, 128], P('groups'), parts along dimension 0
- grad_node_second: float32 [256, 128], P('groups'), parts along dimension 0
- grad_node_gain: float32 [256], P('groups'), parts along dimension 0
There are 2 independent parts, one for each index of `groups`. A program takes and returns all parts, laid end to end along the dimension named above; an argument that names none is the same for every part. Nothing has to cross between parts.
Inputs may be any that keep to these rules, and one draw needn't show every extreme that they name: tile_count[d] counts the live tiles of device d; they are its first tile slots; each count is 32, 16, 8 or 4, and some device has all 32 live. `recv_slot`: -1 marks an empty edge slot.
All inputs are finite; a program needn't handle non-finite values.
Results may differ from a plain program's by a relative error of at most 0.0067.
Values may be sent and summed in bfloat16 or wider, within the bound.
A program may use at most 64 MiB of HBM per device.

v0:
```python
import jax
import jax.numpy as jnp
from jax import lax
from jax.sharding import PartitionSpec as P

NORM_EPSILON = 1e-05


def layer_norm(raw_out):
    row_mean = jnp.mean(raw_out, axis=-1, keepdims=True)
    centred = raw_out - row_mean
    row_var = jnp.mean(centred * centred, axis=-1, keepdims=True)
    inv_scale = lax.rsqrt(row_var + NORM_EPSILON)
    return (centred * inv_scale, inv_scale)


def mlp_back(inputs, first_weight, second_weight, gain_vec, upstream, live_mask):
    pre_act = jnp.dot(inputs, first_weight, preferred_element_type=jnp.float32)
    hidden = jnp.maximum(pre_act, 0.0).astype(jnp.bfloat16)
    raw_out = jnp.dot(hidden, second_weight, preferred_element_type=jnp.float32)
    normed, inv_scale = layer_norm(raw_out)
    weighted = upstream * live_mask
    grad_gain = jnp.sum(weighted * normed, axis=0)
    scaled = weighted * gain_vec
    grad_raw = inv_scale * (
        scaled
        - jnp.mean(scaled, axis=-1, keepdims=True)
        - normed * jnp.mean(scaled * normed, axis=-1, keepdims=True)
    )
    grad_raw = grad_raw.astype(jnp.bfloat16)
    grad_second = jnp.dot(hidden.T, grad_raw, preferred_element_type=jnp.float32)
    grad_hidden = jnp.dot(grad_raw, second_weight.T, preferred_element_type=jnp.float32)
    grad_pre = jnp.where(pre_act > 0.0, grad_hidden, 0.0).astype(jnp.bfloat16)
    grad_first = jnp.dot(inputs.T, grad_pre, preferred_element_type=jnp.float32)
    grad_inputs = jnp.dot(grad_pre, first_weight.T, preferred_element_type=jnp.float32)
    return (grad_inputs, grad_first, grad_second, grad_gain)


def per_device(
    latents,
    saved_sum,
    grad_latents_out,
    edge_latents,
    grad_edges_out,
    recv_slot,
    send_slot,
    tile_recv,
    tile_send,
    tile_count,
    edge_first,
    edge_second,
    edge_gain,
    node_first,
    node_second,
    node_gain,
):
    feat_width = latents.shape[1]
    edge_slots = edge_latents.shape[1]
    row_count = lax.axis_size("row")
    col_count = lax.axis_size("col")
    rep_count = lax.axis_size("rep")
    owned_rows = latents.shape[0]
    block_rows = owned_rows * rep_count
    node_input = jnp.concatenate([latents, saved_sum], axis=1)
    node_live = jnp.ones((owned_rows, 1), jnp.float32)
    grad_node_input, node_first_sum, node_second_sum, node_gain_sum = mlp_back(
        node_input,
        node_first,
        node_second,
        node_gain,
        grad_latents_out.astype(jnp.float32),
        node_live,
    )
    grad_sum = grad_node_input[:, feat_width:].astype(jnp.bfloat16)
    recv_latents, recv_grads = (
        lax.all_gather(latents, ("row", "rep"), axis=0, tiled=True),
        lax.all_gather(grad_sum, ("row", "rep"), axis=0, tiled=True),
    )
    send_latents = lax.all_gather(latents, ("col", "rep"), axis=0, tiled=True)
    recv_blocks = recv_latents.reshape(row_count, block_rows, feat_width)
    grad_blocks = recv_grads.reshape(row_count, block_rows, feat_width)
    send_blocks = send_latents.reshape(col_count, block_rows, feat_width)
    own_count = tile_count[0]
    group_size = 4
    slot_ids = jnp.arange(block_rows, dtype=jnp.int32)
    group_ids = jnp.arange(group_size, dtype=jnp.int32)

    def one_group(group_step, running):
        recv_total, send_total, sum_first, sum_second, sum_gain, grads_out = running
        first_tile = group_step * group_size
        edge_block = lax.dynamic_slice_in_dim(edge_latents, first_tile, group_size, 0)
        grad_block = lax.dynamic_slice_in_dim(grad_edges_out, first_tile, group_size, 0)
        recv_here = lax.dynamic_slice_in_dim(recv_slot, first_tile, group_size, 0)
        send_here = lax.dynamic_slice_in_dim(send_slot, first_tile, group_size, 0)
        trecv_here = lax.dynamic_slice_in_dim(tile_recv, first_tile, group_size, 0)
        tsend_here = lax.dynamic_slice_in_dim(tile_send, first_tile, group_size, 0)
        live_tiles = first_tile + group_ids < own_count
        live_mask = (
            jnp.logical_and(live_tiles[:, None], recv_here >= 0).astype(jnp.float32).reshape(-1, 1)
        )
        recv_pick = (recv_here[:, :, None] == slot_ids).astype(jnp.bfloat16)
        send_pick = (send_here[:, :, None] == slot_ids).astype(jnp.bfloat16)
        recv_rows = jnp.einsum(
            "teb,tbd->ted", recv_pick, recv_blocks[trecv_here], preferred_element_type=jnp.float32
        ).astype(jnp.bfloat16)
        send_rows = jnp.einsum(
            "teb,tbd->ted", send_pick, send_blocks[tsend_here], preferred_element_type=jnp.float32
        ).astype(jnp.bfloat16)
        recv_grad_rows = jnp.einsum(
            "teb,tbd->ted", recv_pick, grad_blocks[trecv_here], preferred_element_type=jnp.float32
        )
        inputs = jnp.concatenate([edge_block, recv_rows, send_rows], axis=2).reshape(
            -1, 3 * feat_width
        )
        flat_grads = grad_block.reshape(-1, feat_width).astype(jnp.float32)
        upstream = flat_grads + recv_grad_rows.reshape(-1, feat_width)
        grad_inputs, grad_first, grad_second, grad_gain = mlp_back(
            inputs, edge_first, edge_second, edge_gain, upstream, live_mask
        )
        new_grads = (
            (flat_grads + grad_inputs[:, :feat_width])
            .astype(jnp.bfloat16)
            .reshape(group_size, edge_slots, feat_width)
        )
        pieces = (
            grad_inputs[:, feat_width:]
            .astype(jnp.bfloat16)
            .reshape(group_size, edge_slots, 2 * feat_width)
        )
        recv_add = jnp.einsum(
            "teb,ted->tbd", recv_pick, pieces[:, :, :feat_width], preferred_element_type=jnp.float32
        )
        send_add = jnp.einsum(
            "teb,ted->tbd", send_pick, pieces[:, :, feat_width:], preferred_element_type=jnp.float32
        )
        recv_total = recv_total.at[trecv_here].add(recv_add)
        send_total = send_total.at[tsend_here].add(send_add)
        grads_out = lax.dynamic_update_slice_in_dim(grads_out, new_grads, first_tile, 0)
        return (
            recv_total,
            send_total,
            sum_first + grad_first,
            sum_second + grad_second,
            sum_gain + grad_gain,
            grads_out,
        )

    initial = (
        jnp.zeros((row_count, block_rows, feat_width), jnp.float32),
        jnp.zeros((col_count, block_rows, feat_width), jnp.float32),
        jnp.zeros(edge_first.shape, jnp.float32),
        jnp.zeros(edge_second.shape, jnp.float32),
        jnp.zeros((feat_width,), jnp.float32),
        grad_edges_out,
    )
    group_steps = (own_count + group_size - 1) // group_size
    recv_total, send_total, edge_first_sum, edge_second_sum, edge_gain_sum, work_result = (
        lax.fori_loop(0, group_steps, one_group, initial)
    )
    recv_part = lax.psum_scatter(
        recv_total.reshape(-1, feat_width), ("row", "rep"), scatter_dimension=0, tiled=True
    )
    send_part = lax.psum_scatter(
        send_total.reshape(-1, feat_width), ("col", "rep"), scatter_dimension=0, tiled=True
    )
    grad_latents = (
        grad_latents_out.astype(jnp.float32)
        + grad_node_input[:, :feat_width]
        + recv_part
        + send_part
    ).astype(jnp.bfloat16)
    totals = lax.psum(
        (
            edge_first_sum,
            edge_second_sum,
            edge_gain_sum,
            node_first_sum,
            node_second_sum,
            node_gain_sum,
        ),
        ("row", "col", "rep"),
    )
    return (
        grad_latents,
        work_result,
        totals[0],
        totals[1],
        totals[2],
        totals[3],
        totals[4],
        totals[5],
    )


def solution(mesh):
    in_specs = (
        P(("groups", "row", "col", "rep"), None),
        P(("groups", "row", "col", "rep"), None),
        P(("groups", "row", "col", "rep"), None),
        P(("groups", "row", "col", "rep"), None, None),
        P(("groups", "row", "col", "rep"), None, None),
        P(("groups", "row", "col", "rep"), None),
        P(("groups", "row", "col", "rep"), None),
        P(("groups", "row", "col", "rep")),
        P(("groups", "row", "col", "rep")),
        P(("groups", "row", "col", "rep")),
        P(),
        P(),
        P(),
        P(),
        P(),
        P(),
    )
    out_specs = (
        P(("groups", "row", "col", "rep"), None),
        P(("groups", "row", "col", "rep"), None, None),
        P("groups", None),
        P("groups", None),
        P("groups"),
        P("groups", None),
        P("groups", None),
        P("groups"),
    )
    return jax.shard_map(
        per_device, mesh=mesh, in_specs=in_specs, out_specs=out_specs, check_vma=False
    )
```

profile of v0, /device:TPU:0, one launch (start us, length us, event | category | flops | bytes accessed | tf_op | source)
XLA Modules:
  0.0 287.1 jit_solution(3019351599939558525)
XLA Ops:
  8.8 0.7 constant_dynamic-update-slice_fusion.2
  9.5 6.4 %all_gather.10 = bf16[256,128]{1,0:T(8,128)(2,1)S(1)} all-gather(bf16[64,128]{1,0:T(8,128)(2,1)} %param.18), channel_id=1, replica_groups=mesh['groups'=2,'row'=4,'col'=2,'rep'=2] {'col','rep'}, dimensions={0}, use_global_device_ids=true | all-gather | bytes 81920 | tf_op jit(solution)/shard_map/all_gather | solution.py:79
  15.9 14.9 %all_gather.9 = bf16[512,128]{1,0:T(8,128)(2,1)S(1)} all-gather(bf16[64,128]{1,0:T(8,128)(2,1)} %param.18), channel_id=1, replica_groups=mesh['groups'=2,'row'=4,'col'=2,'rep'=2] {'row','rep'}, dimensions={0}, use_global_device_ids=true | all-gather | bytes 147456 | tf_op jit(solution)/shard_map/all_gather | solution.py:76
  30.8 0.7 constant_dynamic-update-slice_fusion.1
  32.3 1.0 fusion.36
  33.5 1.4 fusion.30
  34.9 0.8 fusion.25
  35.7 0.9 fusion.19
  37.2 13.9 %all_gather.11 = bf16[512,128]{1,0:T(8,128)(2,1)S(1)} all-gather(bf16[64,128]{1,0:T(8,128)(2,1)S(1)} %slice.49), channel_id=1, replica_groups=mesh['groups'=2,'row'=4,'col'=2,'rep'=2] {'row','rep'}, dimensions={0}, use_global_device_ids=true | all-gather | bytes 147456 | tf_op jit(solution)/shard_map/all_gather | solution.py:77
  51.2 1.0 copy.81
  52.8 0.8 copy-done.3
  53.6 62.7 %while.22 = (s32[]{:T(128)}, f32[4,128,128]{2,1,0:T(8,128)S(1)}, f32[2,128,128]{2,1,0:T(8,128)S(1)}, f32[384,128]{1,0:T(8,128)S(1)}, f32[128,128]{1,0:T(8,128)S(...) while((s32[]{:T(128)}, f32[4,128,128]{2,1,0:T(8,128)S(1)}, ...), condition=%wide.region_12.13_spmd.clone.clone, body=%wide.region_4.12_spmd.clone.clone.sunk | while | flops 289411104 | bytes 17907212 | solution.py:158
  53.7 0.7 fusion.102
  55.1 0.8 and_convert_fusion.2
  58.2 1.0 multiply_reduce_fusion.9
  59.3 0.9 dynamic-slice_convert_fusion.2
  61.4 0.8 multiply_reduce_fusion.10
  63.4 0.8 multiply_convert_fusion.2
  66.3 0.7 scatter_fusion.1
  67.7 0.8 scatter_fusion
  70.8 0.8 and_convert_fusion.2
  73.8 1.0 multiply_reduce_fusion.9
  75.0 0.9 dynamic-slice_convert_fusion.2
  77.1 0.8 multiply_reduce_fusion.10
  79.1 0.8 multiply_convert_fusion.2
  81.9 0.7 scatter_fusion.1
  83.4 0.7 scatter_fusion
  86.5 0.8 and_convert_fusion.2
  89.5 1.0 multiply_reduce_fusion.9
  90.7 0.9 dynamic-slice_convert_fusion.2
  92.7 0.8 multiply_reduce_fusion.10
  94.7 0.8 multiply_convert_fusion.2
  97.6 0.7 scatter_fusion.1
  99.0 0.7 scatter_fusion
  102.1 0.8 and_convert_fusion.2
  105.1 1.0 multiply_reduce_fusion.9
  106.3 0.9 dynamic-slice_convert_fusion.2
  108.4 0.8 multiply_reduce_fusion.10
  110.4 0.8 multiply_convert_fusion.2
  113.3 0.7 scatter_fusion.1
  114.7 0.8 scatter_fusion
  117.9 0.8 fusion.31
  118.7 0.8 fusion.41
  120.3 92.3 %all-reduce = (f32[128]{0:T(128)}, f32[128]{0:T(128)}) all-reduce(f32[128]{0:T(128)S(1)} %copy-done.35, f32[128]{0:T(128)S(1)} %copy-done.32), channel_id=1, replica_groups=mesh['groups'=2,'row'=4,'col'=2,'rep'=2] {'row','col','rep'}, use_global_device_ids=true, to_apply=%region_17.18 | all-reduce | flops 256 | bytes 2048 | tf_op jit(solution)/shard_map/psum | solution.py:172
  212.6 19.8 %reduce-scatter.3.cloned.1.call-done = f32[64,128]{1,0:T(8,128)} async-done(((f32[512,128]{1,0:T(8,128)}), f32[64,128]{1,0:T(8,128)}) %reduce-scatter.3.cloned.1.call-update) | async-done | bytes 32784 | tf_op jit(solution)/shard_map/reduce_scatter | solution.py:160
  232.4 1.4 fusion.29
  233.8 41.8 %all-reduce.4.cloned.1.call-done = (f32[384,128]{1,0:T(8,128)}, f32[128,128]{1,0:T(8,128)}, f32[256,128]{1,0:T(8,128)}, f32[128,128]{1,0:T(8,128)}) async-done(((f32[384,128]{1,0:T(8,128)}, f32[128,128]{1,0:T(8,128)}, f32[256,128]{1,0:T(8,128)}, f32[128,128]{1,0:T(8,128)}), (f32[384,128]{1,0:T(8,128)}, f32[128,128]{1,0:T(8,128)}, f32[256,128]{1,0:T(8,128)}, ...) | async-done | bytes 458768 | tf_op jit(solution)/shard_map/psum | solution.py:172
  275.6 1.6 copy.101
  (292 shorter events, 44.4 us)
Async XLA Ops:
  8.0 24.1 %copy-start = (bf16[256,128]{1,0:T(8,128)(2,1)S(1)}, bf16[256,128]{1,0:T(8,128)(2,1)}, u32[]{:S(2)}) copy-start(bf16[256,128]{1,0:T(8,128)(2,1)} %param.31) | copy-start | bytes 196612
  8.0 43.2 %copy-start.5 = (bf16[32,128,128]{2,1,0:T(8,128)(2,1)S(1)}, bf16[32,128,128]{2,1,0:T(8,128)(2,1)}, u32[]{:S(2)}) copy-start(bf16[32,128,128]{2,1,0:T(8,128)(2,1)} %param.22) | copy-start | bytes 3145732
  8.0 204.6 %reduce-scatter.5.cloned.1.call-start = ((), (), s32[]{:S(2)}) async-start(), calls=%async_computation.3 | async-start | bytes 163840 | tf_op jit(solution)/shard_map/reduce_scatter | solution.py:163
  32.3 3.4 %copy-start.10 = (f32[64,128]{1,0:T(8,128)}, f32[64,128]{1,0:T(8,128)S(1)}, u32[]{:S(2)}) copy-start(f32[64,128]{1,0:T(8,128)S(1)} %fusion.39) | copy-start | bytes 98308
  35.7 0.9 copy-start.16
  37.2 14.0 %copy-start.14 = (f32[64,256]{1,0:T(8,128)}, f32[64,256]{1,0:T(8,128)S(1)}, u32[]{:S(2)}) copy-start(f32[64,256]{1,0:T(8,128)S(1)} %fusion.40) | copy-start | bytes 196612
  52.7 0.9 copy-start.3
  52.7 0.9 copy-start.8
  52.7 0.9 copy-start.28
  52.8 0.9 copy-start.30
  53.6 3.1 %copy-start.6 = (bf16[4,128,128]{2,1,0:T(8,128)(2,1)}, bf16[4,128,128]{2,1,0:T(8,128)(2,1)S(1)}, u32[]{:S(2)}) copy-start(bf16[4,128,128]{2,1,0:T(8,128)(2,1)S(1)} %get-tuple-element.585) | copy-start | bytes 393220 | tf_op jit(solution)/shard_map/while
  54.4 1.5 copy-start.22
  54.4 1.5 copy-start.24
  68.4 0.9 copy-start.7
  68.5 0.9 copy-start.29
  68.5 0.9 copy-start.31
  69.4 3.1 %copy-start.6 = (bf16[4,128,128]{2,1,0:T(8,128)(2,1)}, bf16[4,128,128]{2,1,0:T(8,128)(2,1)S(1)}, u32[]{:S(2)}) copy-start(bf16[4,128,128]{2,1,0:T(8,128)(2,1)S(1)} %get-tuple-element.585) | copy-start | bytes 393220 | tf_op jit(solution)/shard_map/while
  70.1 1.5 copy-start.22
  70.1 1.5 copy-start.24
  84.1 0.9 copy-start.7
  84.1 0.9 copy-start.29
  84.1 0.9 copy-start.31
  85.0 3.1 %copy-start.6 = (bf16[4,128,128]{2,1,0:T(8,128)(2,1)}, bf16[4,128,128]{2,1,0:T(8,128)(2,1)S(1)}, u32[]{:S(2)}) copy-start(bf16[4,128,128]{2,1,0:T(8,128)(2,1)S(1)} %get-tuple-element.585) | copy-start | bytes 393220 | tf_op jit(solution)/shard_map/while
  85.8 1.5 copy-start.22
  85.8 1.5 copy-start.24
  99.8 0.9 copy-start.7
  99.8 0.9 copy-start.29
  99.8 0.9 copy-start.31
  100.7 3.1 %copy-start.6 = (bf16[4,128,128]{2,1,0:T(8,128)(2,1)}, bf16[4,128,128]{2,1,0:T(8,128)(2,1)S(1)}, u32[]{:S(2)}) copy-start(bf16[4,128,128]{2,1,0:T(8,128)(2,1)S(1)} %get-tuple-element.585) | copy-start | bytes 393220 | tf_op jit(solution)/shard_map/while
  101.4 1.5 copy-start.22
  101.4 1.5 copy-start.24
  115.4 0.9 copy-start.7
  115.4 0.9 copy-start.29
  115.5 0.9 copy-start.31
  116.3 0.8 copy-start.2
  116.4 1.4 copy-start.4
  116.4 1.4 copy-start.9
  117.0 115.4 %reduce-scatter.3.cloned.1.call-start = ((), (), s32[]{:S(2)}) async-start(), calls=%async_computation.2 | async-start | bytes 294912 | tf_op jit(solution)/shard_map/reduce_scatter | solution.py:160
  117.1 0.8 copy-start.11
  117.1 0.8 copy-start.17
  117.1 115.3 %copy-start.18 = (bf16[64,128]{1,0:T(8,128)(2,1)S(1)}, bf16[64,128]{1,0:T(8,128)(2,1)}, u32[]{:S(2)}) copy-start(bf16[64,128]{1,0:T(8,128)(2,1)} %param.20) | copy-start | bytes 49156
  117.8 0.9 copy-start.13
  117.8 0.9 copy-start.20
  117.8 157.8 %all-reduce.4.cloned.1.call-start = ((), (), s32[]{:S(2)}) async-start(), calls=%async_computation.4 | async-start | bytes 917504 | tf_op jit(solution)/shard_map/psum | solution.py:172
  119.6 112.9 %copy-start.15 = (f32[64,256]{1,0:T(8,128)S(1)}, f32[64,256]{1,0:T(8,128)}, u32[]{:S(2)}) copy-start(f32[64,256]{1,0:T(8,128)} %copy-done.14) | copy-start | bytes 196612
  275.6 1.7 copy-start.27
  277.2 0.9 copy-start.21
  278.2 0.9 copy-start.26
  (21 other events, 13.3 us)
Sparse Core Ops, SparseCore 0:
  117.1 82.4 reduce-scatter.4
  202.0 30.3 reduce-scatter.2
Sparse Core Ops, SparseCore 1:
  122.6 152.9 all-reduce.3
where the time goes:
time: 290 us; the launch traced here: 287 us
  blocking collectives  128 us (44%)
  waiting for transfers between devices  62.3 us (21%)
  local copies, waits for them, and re-layouts  35.7 us (12%)
  other arithmetic  26.5 us (9%)
  matrix products  17.3 us (6%)
  between operations  16.5 us (6%)
    psum x1, blocking collectives, per_device(): lax.psum((edge_first_sum, edge_second_sum, edge_gain_sum, node_first_sum,...  92.3 us
    psum x1, waiting for transfers between devices, per_device(): lax.psum((edge_first_sum, edge_second_sum, edge_gain_sum, node_first_sum,...  41.8 us
    reduce_scatter x1, waiting for transfers between devices, per_device(): lax.psum_scatter(recv_total.reshape(-1, feat_width), ('row', 'rep'), scat...  19.8 us
    all_gather x1, blocking collectives, per_device(): lax.all_gather(latents, ('row', 'rep'), axis=0, tiled=True)  14.9 us
    all_gather x1, blocking collectives, per_device(): lax.all_gather(grad_sum, ('row', 'rep'), axis=0, tiled=True)  13.9 us
    while x84, local copies, waits for them, and re-layouts  9.91 us
    unnamed x58, local copies, waits for them, and re-layouts  9.06 us
    all_gather x1, blocking collectives, per_device(): send_latents = lax.all_gather(latents, ('col', 'rep'), axis=0, tiled=True)  6.41 us
  transfers between devices with their start and end apart: 3, of which 2 were waited for; matrix products, arithmetic and copies ran while one was open for 1% of the time, Pallas kernels for 0%

commit v1 on v0

v1 whole, which is shorter than its diff:
```python
import functools

import jax
import jax.numpy as jnp
from jax import lax
from jax.experimental import pallas as pl
from jax.experimental.pallas import tpu as pltpu
from jax.sharding import PartitionSpec as P

NORM_EPSILON = 1e-05
MESH = pl.DeviceIdType.MESH
F32 = jnp.float32
BF16 = jnp.bfloat16
GROUP = 8
PAIR = 2


def dot(a, b):
    return jnp.dot(a, b, preferred_element_type=F32)


def dot_nt(a, b):
    return lax.dot_general(a, b, (((1,), (1,)), ((), ())), preferred_element_type=F32)


def norm_back(raw, weighted, gain):
    row_mean = jnp.mean(raw, axis=-1, keepdims=True)
    centred = raw - row_mean
    row_var = jnp.mean(centred * centred, axis=-1, keepdims=True)
    inv_scale = lax.rsqrt(row_var + NORM_EPSILON)
    normed = centred * inv_scale
    gain_term = weighted * normed
    scaled = weighted * gain
    mean_scaled = jnp.mean(scaled, axis=-1, keepdims=True)
    mean_both = jnp.mean(scaled * normed, axis=-1, keepdims=True)
    grad_raw = inv_scale * (scaled - mean_scaled - normed * mean_both)
    return grad_raw.astype(BF16), gain_term


def node_kernel(
    nr, nc, lat_ref, sum_ref, glo_ref, first_ref, second_ref, gain_ref,
    rlat_ref, rgrad_ref, slat_ref, base_ref, wn_ref,
    gs_buf, lat_send, lat_recv, gs_send, gs_recv, sl_send, sl_recv,
):
    row, col, rep = lax.axis_index("row"), lax.axis_index("col"), lax.axis_index("rep")
    rows, width = lat_ref.shape
    nrr, ncr = nr * 2, nc * 2
    mine_r, mine_c = row * 2 + rep, col * 2 + rep

    def r_dev(k):
        other = lax.rem(mine_r + k, nrr)
        return {"row": lax.div(other, 2), "rep": lax.rem(other, 2)}

    def c_dev(k):
        other = lax.rem(mine_c + k, ncr)
        return {"col": lax.div(other, 2), "rep": lax.rem(other, 2)}

    barrier = pltpu.get_barrier_semaphore()
    for k in range(1, nrr):
        pl.semaphore_signal(barrier, inc=1, device_id=r_dev(k), device_id_type=MESH)
    for k in range(1, ncr):
        pl.semaphore_signal(barrier, inc=1, device_id=c_dev(k), device_id_type=MESH)
    pl.semaphore_wait(barrier, nrr + ncr - 2)

    r_here = pl.ds(pl.multiple_of(mine_r * rows, 16), rows)
    c_here = pl.ds(pl.multiple_of(mine_c * rows, 16), rows)
    lat_copies, sl_copies, gs_copies = [], [], []
    for k in range(1, nrr):
        lat_copies.append(pltpu.make_async_remote_copy(
            src_ref=lat_ref, dst_ref=rlat_ref.at[r_here], send_sem=lat_send.at[k],
            recv_sem=lat_recv.at[k], device_id=r_dev(k), device_id_type=MESH))
        lat_copies[-1].start()
    for k in range(1, ncr):
        sl_copies.append(pltpu.make_async_remote_copy(
            src_ref=lat_ref, dst_ref=slat_ref.at[c_here], send_sem=sl_send.at[k],
            recv_sem=sl_recv.at[k], device_id=c_dev(k), device_id_type=MESH))
        sl_copies[-1].start()

    lat = lat_ref[...]
    inputs = jnp.concatenate([lat, sum_ref[...]], axis=1)
    pre = dot(inputs, first_ref[...])
    hidden = jnp.maximum(pre, 0.0).astype(BF16)
    raw = dot(hidden, second_ref[...])
    upstream = glo_ref[...].astype(F32)
    grad_raw, gain_term = norm_back(raw, upstream, gain_ref[...])
    grad_hidden = dot_nt(grad_raw, second_ref[...])
    grad_pre = jnp.where(pre > 0.0, grad_hidden, 0.0).astype(BF16)
    grad_in = dot_nt(grad_pre, first_ref[...])
    grad_sum = grad_in[:, width:].astype(BF16)
    gs_buf[...] = grad_sum
    for k in range(1, nrr):
        gs_copies.append(pltpu.make_async_remote_copy(
            src_ref=gs_buf, dst_ref=rgrad_ref.at[r_here], send_sem=gs_send.at[k],
            recv_sem=gs_recv.at[k], device_id=r_dev(k), device_id_type=MESH))
        gs_copies[-1].start()
    rlat_ref[r_here, :] = lat
    rgrad_ref[r_here, :] = grad_sum
    slat_ref[c_here, :] = lat
    base_ref[...] = upstream + grad_in[:, :width]
    w1 = first_ref.shape[0]
    w2 = w1 + second_ref.shape[0]
    wn_ref[0:w1, :] = dot(inputs.T, grad_pre).astype(BF16)
    wn_ref[w1:w2, :] = dot(hidden.T, grad_raw).astype(BF16)
    wn_ref[w2:w2 + 16, :] = jnp.broadcast_to(
        jnp.sum(gain_term, axis=0, keepdims=True), (16, width)).astype(BF16)
    for copy in lat_copies + sl_copies + gs_copies:
        copy.wait_recv()
    for copy in lat_copies + sl_copies + gs_copies:
        copy.wait_send()


def edge_kernel(
    nr, nc, half_rows, trecv_ref, tsend_ref, count_ref,
    edge_ref, grad_ref, rslot_ref, sslot_ref, rlat_ref, rgrad_ref, slat_ref,
    first_ref, second_ref, gain_ref, wn_ref,
    out_ref, pack_ref,
    cat, first_t, second_t, acc_r, acc_s, acc_first, acc_second, acc_gain,
):
    step = pl.program_id(0)
    width = edge_ref.shape[2]
    slots = edge_ref.shape[1]
    block = rlat_ref.shape[1]
    count = count_ref[0]

    @pl.when(step == 0)
    def _():
        cat[:, :, 0:width] = rlat_ref[...]
        cat[:, :, width:2 * width] = rgrad_ref[...]
        first_t[...] = first_ref[0:width, :].T
        second_t[...] = second_ref[...].T
        acc_r[...] = jnp.zeros_like(acc_r)
        acc_s[...] = jnp.zeros_like(acc_s)
        acc_first[...] = jnp.zeros_like(acc_first)
        acc_second[...] = jnp.zeros_like(acc_second)
        acc_gain[...] = jnp.zeros_like(acc_gain)

    live_step = step * GROUP < count

    @pl.when(jnp.logical_not(live_step))
    def _():
        out_ref[...] = grad_ref[...]

    @pl.when(live_step)
    def _():
        rcols = rslot_ref[...].T
        scols = sslot_ref[...].T
        lanes = lax.broadcasted_iota(jnp.int32, (slots, block), 1)
        first = first_ref[...]
        gain = gain_ref[...]
        for pair in range(GROUP // PAIR):
            recv_rows, send_rows, weighted, picks, flats = [], [], [], [], []
            for t in range(pair * PAIR, (pair + 1) * PAIR):
                tile = step * GROUP + t
                rcol = jnp.broadcast_to(rcols[:, t:t + 1], (slots, block))
                scol = jnp.broadcast_to(scols[:, t:t + 1], (slots, block))
                rpick = jnp.where(rcol == lanes, 1.0, 0.0).astype(BF16)
                spick = jnp.where(scol == lanes, 1.0, 0.0).astype(BF16)
                from_recv = dot(rpick, cat[trecv_ref[tile]])
                from_send = dot(spick, slat_ref[tsend_ref[tile]])
                recv_rows.append(from_recv[:, 0:width].astype(BF16))
                send_rows.append(from_send.astype(BF16))
                flat = grad_ref[t].astype(F32)
                least = jnp.where(tile < count, 0, block)
                weighted.append(jnp.where(rcol >= least, flat + from_recv[:, width:], 0.0))
                flats.append(flat)
                picks.append(jnp.concatenate([rpick, spick], axis=1))
            edges = edge_ref[pair * PAIR:(pair + 1) * PAIR].reshape(PAIR * slots, width)
            inputs = jnp.concatenate(
                [edges, jnp.concatenate(recv_rows, axis=0), jnp.concatenate(send_rows, axis=0)],
                axis=1)
            pre = dot(inputs, first)
            hidden = jnp.maximum(pre, 0.0).astype(BF16)
            raw = dot(hidden, second_ref[...])
            grad_raw, gain_term = norm_back(raw, jnp.concatenate(weighted, axis=0), gain)
            acc_gain[...] += jnp.sum(gain_term.reshape(-1, 8, width), axis=0)
            grad_hidden = dot(grad_raw, second_t[...])
            grad_pre = jnp.where(pre > 0.0, grad_hidden, 0.0).astype(BF16)
            acc_second[...] += dot(hidden.T, grad_raw)
            grad_in = dot(grad_pre, first_t[...])
            grad_pre_t = grad_pre.T
            acc_first[:, 0:width] += dot(grad_pre_t, edges)
            for i in range(PAIR):
                t = pair * PAIR + i
                tile = step * GROUP + t
                out_ref[t] = (flats[i] + grad_in[i * slots:(i + 1) * slots]).astype(BF16)
                both = dot(grad_pre_t[:, i * slots:(i + 1) * slots], picks[i])
                acc_r[trecv_ref[tile]] += both[:, 0:block]
                acc_s[tsend_ref[tile]] += both[:, block:]

    @pl.when(step == pl.num_programs(0) - 1)
    def _():
        half = block // 2
        recv_w = first_ref[width:2 * width, :]
        send_w = first_ref[2 * width:3 * width, :]
        first_r = acc_first[:, width:2 * width]
        for b in range(nr):
            summed = acc_r[b].astype(BF16)
            total = dot(recv_w, summed).T.astype(BF16)
            first_r += dot(summed, rlat_ref[b])
            for h in range(2):
                pack_ref[h, b * half:(b + 1) * half, :] = total[h * half:(h + 1) * half]
        first_s = acc_first[:, 2 * width:3 * width]
        for b in range(nc):
            summed = acc_s[b].astype(BF16)
            total = dot(send_w, summed).T.astype(BF16)
            first_s += dot(summed, slat_ref[b])
            for h in range(2):
                pack_ref[h, (nr + b) * half:(nr + b + 1) * half, :] = total[h * half:(h + 1) * half]
        w0 = (nr + nc) * half
        hid = second_ref.shape[0]
        pack_ref[0, w0:w0 + width, :] = acc_first[:, 0:width].T.astype(BF16)
        pack_ref[0, w0 + width:w0 + 2 * width, :] = first_r.T.astype(BF16)
        pack_ref[0, w0 + 2 * width:w0 + 3 * width, :] = first_s.T.astype(BF16)
        pack_ref[0, w0 + 3 * width:w0 + 3 * width + hid, :] = acc_second[...].astype(BF16)
        used = 3 * width + hid
        if half_rows > used:
            pack_ref[0, w0 + used:w0 + half_rows, :] = jnp.zeros((half_rows - used, width), BF16)
        nw = wn_ref.shape[0]
        pack_ref[1, w0:w0 + nw, :] = wn_ref[...]
        pack_ref[1, w0 + nw:w0 + nw + 16, :] = jnp.broadcast_to(
            jnp.sum(acc_gain[...], axis=0, keepdims=True), (16, width)).astype(BF16)
        pack_ref[1, w0 + nw + 16:w0 + half_rows, :] = jnp.zeros(
            (half_rows - nw - 16, width), BF16)


def sum_kernel(
    nr, nc, chunk, pack_ref, base_ref,
    glat_ref, ef_ref, es_ref, eg_ref, nf_ref, ns_ref, ng_ref,
    buf, part, rbuf, sbuf, wbuf, wfin,
    p_send, p_recv, w_send, w_recv, r_send, r_recv, s_send, s_recv,
    a_send, a_recv, f_send, f_recv,
):
    row, col, rep = lax.axis_index("row"), lax.axis_index("col"), lax.axis_index("rep")
    chips = nr * nc
    here = row * nc + col
    other_rep = 1 - rep
    rows = base_ref.shape[0]
    w0 = (nr + nc) * rows
    half_rows = chunk * chips
    twin = {"rep": other_rep}

    def chip(k):
        other = lax.rem(here + k, chips)
        return other, {"row": lax.div(other, nc), "col": lax.rem(other, nc)}

    barrier = pltpu.get_barrier_semaphore()
    pl.semaphore_signal(barrier, inc=1, device_id=twin, device_id_type=MESH)
    for k in range(1, chips):
        pl.semaphore_signal(barrier, inc=1, device_id=chip(k)[1], device_id_type=MESH)
    pl.semaphore_wait(barrier, chips)

    def send(src, dst, send_sem, recv_sem, device):
        copy = pltpu.make_async_remote_copy(
            src_ref=src, dst_ref=dst, send_sem=send_sem, recv_sem=recv_sem,
            device_id=device, device_id_type=MESH)
        copy.start()
        return copy

    w_part, n_part = pl.ds(w0, half_rows), pl.ds(0, w0)
    p_w = send(pack_ref.at[other_rep, w_part], buf.at[w_part], p_send.at[0], p_recv.at[0], twin)
    p_n = send(pack_ref.at[other_rep, n_part], buf.at[n_part], p_send.at[1], p_recv.at[1], twin)

    def at_chunk(index):
        return pl.ds(pl.multiple_of(index * chunk, 16), chunk)

    def at_part(offset, index, size):
        return pl.ds(pl.multiple_of(offset + index * size, 16), size)

    p_w.wait_recv()
    part[w_part, :] = (pack_ref[rep, w_part, :].astype(F32) + buf[w_part, :].astype(F32)).astype(BF16)
    w_copies = []
    for k in range(1, chips):
        other, device = chip(k)
        w_copies.append(send(part.at[at_part(w0, other, chunk)], wbuf.at[k],
                             w_send.at[k], w_recv.at[k], device))
    p_n.wait_recv()
    part[n_part, :] = (pack_ref[rep, n_part, :].astype(F32) + buf[n_part, :].astype(F32)).astype(BF16)
    r_copies, s_copies = [], []
    for k in range(1, nr):
        other = lax.rem(row + k, nr)
        r_copies.append(send(part.at[at_part(0, other, rows)], rbuf.at[k],
                             r_send.at[k], r_recv.at[k], {"row": other}))
    for k in range(1, nc):
        other = lax.rem(col + k, nc)
        s_copies.append(send(part.at[at_part(nr * rows, other, rows)], sbuf.at[k],
                             s_send.at[k], s_recv.at[k], {"col": other}))

    total = part[at_part(w0, here, chunk), :].astype(F32)
    for k in range(1, chips):
        w_copies[k - 1].wait_recv()
        total += wbuf[k].astype(F32)
    wfin[rep, at_chunk(here), :] = total.astype(BF16)
    mine = wfin.at[rep, at_chunk(here)]
    a_copies = [send(mine, mine, a_send.at[k], a_recv.at[k], chip(k)[1]) for k in range(1, chips)]
    f_copies = [send(mine, mine, f_send.at[0], f_recv.at[0], twin)]

    grads = base_ref[...] + part[at_part(0, row, rows), :].astype(F32)
    grads += part[at_part(nr * rows, col, rows), :].astype(F32)
    for k in range(1, nr):
        r_copies[k - 1].wait_recv()
        grads += rbuf[k].astype(F32)
    for k in range(1, nc):
        s_copies[k - 1].wait_recv()
        grads += sbuf[k].astype(F32)
    glat_ref[...] = grads.astype(BF16)

    for k in range(1, chips):
        a_copies[k - 1].wait_recv()
        source = lax.rem(here + chips - k, chips)
        passed = wfin.at[rep, at_chunk(source)]
        f_copies.append(send(passed, passed, f_send.at[k], f_recv.at[k], twin))
    for copy in f_copies:
        copy.wait_recv()
    nef, nes = ef_ref.shape[0], es_ref.shape[0]
    ef_ref[...] = wfin[0, 0:nef, :].astype(F32)
    es_ref[...] = wfin[0, nef:nef + nes, :].astype(F32)
    nnf, nns = nf_ref.shape[0], ns_ref.shape[0]
    nf_ref[...] = wfin[1, 0:nnf, :].astype(F32)
    ns_ref[...] = wfin[1, nnf:nnf + nns, :].astype(F32)
    gains = wfin[1, nnf + nns:nnf + nns + 32, :].astype(F32)
    ng_ref[...] = gains[0:1]
    eg_ref[...] = gains[16:17]
    for copy in [p_w, p_n] + w_copies + r_copies + s_copies + a_copies + f_copies:
        copy.wait_send()


def per_device(
    latents, saved_sum, grad_latents_out, edge_latents, grad_edges_out, recv_slot, send_slot,
    tile_recv, tile_send, tile_count, edge_first, edge_second, edge_gain,
    node_first, node_second, node_gain,
):
    nr, nc = lax.axis_size("row"), lax.axis_size("col")
    rows, width = latents.shape
    tiles, slots, _ = edge_latents.shape
    block = rows * 2
    chips = nr * nc
    vmem = pl.BlockSpec(memory_space=pltpu.VMEM)
    dma = pltpu.SemaphoreType.DMA
    weight_rows = edge_first.shape[0] + edge_second.shape[0]
    node_rows = node_first.shape[0] + node_second.shape[0]
    chunk = -(-max(weight_rows, node_rows + 32) // (16 * chips)) * 16
    half_rows = chunk * chips
    nrr, ncr = nr * 2, nc * 2
    shape = jax.ShapeDtypeStruct

    rlat, rgrad, slat, base, wn = pl.pallas_call(
        functools.partial(node_kernel, nr, nc),
        out_shape=(
            shape((nrr * rows, width), BF16), shape((nrr * rows, width), BF16),
            shape((ncr * rows, width), BF16), shape((rows, width), F32),
            shape((node_rows + 16, width), BF16),
        ),
        in_specs=[vmem] * 6,
        out_specs=(vmem,) * 5,
        scratch_shapes=[pltpu.VMEM((rows, width), BF16),
                        dma((nrr,)), dma((nrr,)), dma((nrr,)), dma((nrr,)), dma((ncr,)), dma((ncr,))],
        compiler_params=pltpu.CompilerParams(
            collective_id=0, has_side_effects=True, vmem_limit_bytes=32 << 20),
    )(latents, saved_sum, grad_latents_out, node_first, node_second, node_gain.reshape(1, -1))

    def whole(*dims):
        return pl.BlockSpec(dims, lambda i, *_: (0,) * len(dims))

    tiled = pl.BlockSpec((GROUP, slots, width), lambda i, *_: (i, 0, 0))
    slotted = pl.BlockSpec((GROUP, slots), lambda i, *_: (i, 0))
    pack_rows = (nr + nc) * rows + half_rows
    grads_out, pack = pl.pallas_call(
        functools.partial(edge_kernel, nr, nc, half_rows),
        out_shape=(shape(edge_latents.shape, BF16), shape((2, pack_rows, width), BF16)),
        grid_spec=pltpu.PrefetchScalarGridSpec(
            num_scalar_prefetch=3,
            grid=(tiles // GROUP,),
            in_specs=[
                tiled, tiled, slotted, slotted,
                whole(nr, block, width), whole(nr, block, width), whole(nc, block, width),
                whole(*edge_first.shape), whole(*edge_second.shape), whole(1, width),
                whole(node_rows + 16, width),
            ],
            out_specs=(tiled, whole(2, pack_rows, width)),
            scratch_shapes=[
                pltpu.VMEM((nr, block, 2 * width), BF16),
                pltpu.VMEM((edge_first.shape[1], width), BF16),
                pltpu.VMEM((width, edge_second.shape[0]), BF16),
                pltpu.VMEM((nr, edge_first.shape[1], block), F32),
                pltpu.VMEM((nc, edge_first.shape[1], block), F32),
                pltpu.VMEM((edge_first.shape[1], edge_first.shape[0]), F32),
                pltpu.VMEM(edge_second.shape, F32),
                pltpu.VMEM((8, width), F32),
            ],
        ),
        compiler_params=pltpu.CompilerParams(
            dimension_semantics=("arbitrary",), vmem_limit_bytes=40 << 20),
    )(
        tile_recv, tile_send, tile_count, edge_latents, grad_edges_out, recv_slot, send_slot,
        rlat.reshape(nr, block, width), rgrad.reshape(nr, block, width),
        slat.reshape(nc, block, width), edge_first, edge_second, edge_gain.reshape(1, -1), wn,
    )

    outs = pl.pallas_call(
        functools.partial(sum_kernel, nr, nc, chunk),
        out_shape=(
            shape((rows, width), BF16), shape(edge_first.shape, F32),
            shape(edge_second.shape, F32), shape((1, width), F32),
            shape(node_first.shape, F32), shape(node_second.shape, F32), shape((1, width), F32),
        ),
        in_specs=[vmem] * 2,
        out_specs=(vmem,) * 7,
        scratch_shapes=[
            pltpu.VMEM((pack_rows, width), BF16), pltpu.VMEM((pack_rows, width), BF16),
            pltpu.VMEM((nr, rows, width), BF16), pltpu.VMEM((nc, rows, width), BF16),
            pltpu.VMEM((chips, chunk, width), BF16), pltpu.VMEM((2, half_rows, width), BF16),
            dma((2,)), dma((2,)), dma((chips,)), dma((chips,)), dma((nr,)), dma((nr,)),
            dma((nc,)), dma((nc,)), dma((chips,)), dma((chips,)), dma((chips,)), dma((chips,)),
        ],
        compiler_params=pltpu.CompilerParams(
            collective_id=1, has_side_effects=True, vmem_limit_bytes=40 << 20),
    )(pack, base)
    grad_latents, ef, es, eg, nf, ns, ng = outs
    return (grad_latents, grads_out, ef, es, eg.reshape(-1), nf, ns, ng.reshape(-1))


def solution(mesh):
    spread = ("groups", "row", "col", "rep")
    two, three, one = P(spread, None), P(spread, None, None), P(spread)
    in_specs = (two, two, two, three, three, two, two, one, one, one) + (P(),) * 6
    out_specs = (
        two, three, P("groups", None), P("groups", None), P("groups"),
        P("groups", None), P("groups", None), P("groups"),
    )
    return jax.shard_map(
        per_device, mesh=mesh, in_specs=in_specs, out_specs=out_specs, check_vma=False
    )
```

time: 290 us -> 59 us (0.20)
  blocking collectives: 128 us -> 0 us
  waiting for transfers between devices: 62.3 us -> 0 us
  Pallas kernels: 0 us -> 44.8 us
  other arithmetic: 26.5 us -> 0 us
  local copies, waits for them, and re-layouts: 35.7 us -> 11.7 us
  matrix products: 17.3 us -> 0 us
  between operations: 16.5 us -> 1.42 us
    psum x1 -> x0, blocking collectives: 92.3 us -> none  [per_device(): lax.psum((edge_first_sum, edge_second_sum, edge_gain_sum, node_first_sum,...]
    pallas_call x0 -> x3, Pallas kernels: none -> 44.8 us  [the longest x1 17.5 us: per_device(): pl.pallas_call(functools.partial(edge_kernel, nr, nc, half_rows), out_sha...]
    psum x1 -> x0, waiting for transfers between devices: 41.8 us -> none  [per_device(): lax.psum((edge_first_sum, edge_second_sum, edge_gain_sum, node_first_sum,...]
    all_gather x3 -> x0, blocking collectives: 35.2 us -> none  [the longest x1 14.9 us: per_device(): lax.all_gather(latents, ('row', 'rep'), axis=0, tiled=True)]
    reduce_scatter x2 -> x0, waiting for transfers between devices: 19.8 us -> none  [the longest x1 19.8 us: per_device(): lax.psum_scatter(recv_total.reshape(-1, feat_width), ('row', 'rep'), scat...]
    dot_general x50 -> x0, matrix products: 17.3 us -> none  [the longest x4 4.12 us: one_group(): jnp.einsum('teb,tbd->ted', recv_pick, grad_blocks[trecv_here], preferred_...]
    convert_element_type x18 -> x0, other arithmetic: 12.2 us -> none  [the longest x5 3.88 us: mlp_back(): grad_raw = grad_raw.astype(jnp.bfloat16)]
    while x84 -> x0, local copies, waits for them, and re-layouts: 9.91 us -> none
  transfers between devices with their start and end apart: 3 -> 0, of which waited for: 2 -> 0; matrix products, arithmetic and copies ran while one was open for 1% -> 0% of each run, Pallas kernels for 0% -> 0%
where the time goes in v1:
time: 59 us; the launch traced here: 57.9 us
  Pallas kernels  44.8 us (76%)
  local copies, waits for them, and re-layouts  11.7 us (20%)
  between operations  1.42 us (2%)
    pallas_call x1, Pallas kernels, per_device(): pl.pallas_call(functools.partial(edge_kernel, nr, nc, half_rows), out_sha...  17.5 us
    pallas_call x1, Pallas kernels, per_device(): pl.pallas_call(functools.partial(sum_kernel, nr, nc, chunk), out_shape=(s...  15.2 us
    pallas_call x1, Pallas kernels, per_device(): pl.pallas_call(functools.partial(node_kernel, nr, nc), out_shape=(shape((...  12.1 us
    unnamed x37, local copies, waits for them, and re-layouts  11.7 us

profile of v1, /device:TPU:0, one launch (start us, length us, event | category | flops | bytes accessed | tf_op | source)
XLA Modules:
  0.0 57.9 jit_solution(10792859404309693118)
XLA Ops:
  0.6 0.0 copy-start.2
  1.3 0.0 copy-start.3
  1.3 0.8 %copy-done.3 = bf16[256,128]{1,0:T(8,128)(2,1)S(1)} copy-done((bf16[256,128]{1,0:T(8,128)(2,1)S(1)}, bf16[256,128]{1,0:T(8,128)(2,1)}, u32[]{:S(2)}) %copy-start.3) | copy-done | bytes 65560
  2.2 0.0 copy-start.5
  2.2 0.8 %copy-done.5 = bf16[128,128]{1,0:T(8,128)(2,1)S(1)} copy-done((bf16[128,128]{1,0:T(8,128)(2,1)S(1)}, bf16[128,128]{1,0:T(8,128)(2,1)}, u32[]{:S(2)}) %copy-start.5) | copy-done | bytes 32792
  2.9 0.0 copy-start.8
  2.9 0.7 %copy-done.8 = bf16[64,128]{1,0:T(8,128)(2,1)S(1)} copy-done((bf16[64,128]{1,0:T(8,128)(2,1)S(1)}, bf16[64,128]{1,0:T(8,128)(2,1)}, u32[]{:S(2)}) %copy-start.8) | copy-done | bytes 16408
  3.6 0.0 copy-start.9
  3.6 0.7 %copy-done.9 = bf16[64,128]{1,0:T(8,128)(2,1)S(1)} copy-done((bf16[64,128]{1,0:T(8,128)(2,1)S(1)}, bf16[64,128]{1,0:T(8,128)(2,1)}, u32[]{:S(2)}) %copy-start.9) | copy-done | bytes 16408
  4.4 0.0 copy-start.10
  4.4 0.7 %copy-done.10 = bf16[64,128]{1,0:T(8,128)(2,1)S(1)} copy-done((bf16[64,128]{1,0:T(8,128)(2,1)S(1)}, bf16[64,128]{1,0:T(8,128)(2,1)}, u32[]{:S(2)}) %copy-start.10) | copy-done | bytes 16408
  5.1 0.0 copy-start.11
  5.1 0.7 %copy-done.11 = f32[128]{0:T(128)S(1)} copy-done((f32[128]{0:T(128)S(1)}, f32[128]{0:T(128)}, u32[]{:S(2)}) %copy-start.11) | copy-done | bytes 536
  5.7 0.0 copy-start.4
  5.7 0.0 copy-start.6
  5.7 0.0 copy-start.7
  5.7 12.1 %shard_map.215 = (bf16[512,128]{1,0:T(8,128)(2,1)S(1)}, bf16[512,128]{1,0:T(8,128)(2,1)S(1)}, bf16[256,128]{1,0:T(8,128)(2,1)S(1)}, f32[64,128]{1,0:T(8,128)S(1)}, bf16[400,128]{1,0:T(8,128)(2,1)S(1)}) custom-call(bf16[64,128]{1,0:T(8,128)(2,1)S(1)} %copy-done.8, bf16[64,128]{1,0:T(8,128)(2,1)S(1)} %copy-done.9, bf16[64,128]{1,0:T(8,128)(2,1)S(1)} %copy-done.10, ...), custom_call_target="tpu_custom_call" | custom-call | tf_op jit(solution)/shard_map/pallas_call | solution.py:346
  17.8 0.0 copy-start.12
  17.8 0.0 copy-start.13
  17.8 0.0 copy-start.14
  17.9 0.0 copy-done.2
  17.9 0.0 copy-done.4
  17.9 0.0 copy-done.6
  17.9 0.0 copy-done.7
  17.9 0.6 %copy-done.12 = s32[32]{0:T(128)S(1)} copy-done((s32[32]{0:T(128)S(1)}, s32[32]{0:T(128)}, u32[]{:S(2)}) %copy-start.12) | copy-done | bytes 152
  18.5 0.0 copy-done.13
  18.5 0.0 copy-done.14
  18.5 0.0 copy-start
  18.5 1.2 %copy-done = bf16[32,128,128]{2,1,0:T(8,128)(2,1)S(1)} copy-done((bf16[32,128,128]{2,1,0:T(8,128)(2,1)S(1)}, bf16[32,128,128]{2,1,0:T(8,128)(2,1)}, u32[]{:S(2)}) %copy-start) | copy-done | bytes 1048600
  19.7 0.0 copy-start.1
  19.7 1.2 %copy-done.1 = bf16[32,128,128]{2,1,0:T(8,128)(2,1)S(1)} copy-done((bf16[32,128,128]{2,1,0:T(8,128)(2,1)S(1)}, bf16[32,128,128]{2,1,0:T(8,128)(2,1)}, u32[]{:S(2)}) %copy-start.1) | copy-done | bytes 1048600
  21.0 17.5 %shard_map.216 = (bf16[32,128,128]{2,1,0:T(8,128)(2,1)}, bf16[2,896,128]{2,1,0:T(8,128)(2,1)S(1)}) custom-call(s32[32]{0:T(128)S(1)} %copy-done.12, s32[32]{0:T(128)S(1)} %copy-done.13, s32[1]{0:T(128)S(6)} %copy.31.count_ref, bf16[32,128,128]{2,1,0:T(8,128)(2,1)S(1)} %copy-done, bf16[32,128,128]{2,1,0:T(8,128)(2,1)S(1)} %copy-done.1, ...), custom_call_target="tpu_custom_call" | custom-call | tf_op jit(solution)/shard_map/pallas_call | solution.py:367
  38.5 15.2 %shard_map.217 = (bf16[64,128]{1,0:T(8,128)(2,1)S(1)}, f32[384,128]{1,0:T(8,128)S(1)}, f32[128,128]{1,0:T(8,128)S(1)}, f32[1,128]{1,0:T(1,128)S(1)}, f32[256,128...) custom-call(bf16[2,896,128]{2,1,0:T(8,128)(2,1)S(1)} %get-tuple-element.26.pack_ref, ...), custom_call_target="tpu_custom_call" | custom-call | tf_op jit(solution)/shard_map/pallas_call | solution.py:399
  53.7 0.6 %copy.32 = bf16[64,128]{1,0:T(8,128)(2,1)} copy(bf16[64,128]{1,0:T(8,128)(2,1)S(1)} %get-tuple-element.44) | data formatting | bytes 32768
  54.3 0.7 %copy.33 = f32[384,128]{1,0:T(8,128)} copy(f32[384,128]{1,0:T(8,128)S(1)} %get-tuple-element.46) | data formatting | bytes 393216
  54.9 0.6 %copy.34 = f32[128,128]{1,0:T(8,128)} copy(f32[128,128]{1,0:T(8,128)S(1)} %get-tuple-element.47) | data formatting | bytes 131072
  55.6 0.5 copy.35
  56.1 0.7 %copy.36 = f32[256,128]{1,0:T(8,128)} copy(f32[256,128]{1,0:T(8,128)S(1)} %get-tuple-element.49) | data formatting | bytes 262144
  56.7 0.6 %copy.37 = f32[128,128]{1,0:T(8,128)} copy(f32[128,128]{1,0:T(8,128)S(1)} %get-tuple-element.50) | data formatting | bytes 131072
  57.4 0.5 copy.38
Async XLA Ops:
  0.6 17.2 %copy-start.2 = (bf16[384,128]{1,0:T(8,128)(2,1)S(1)}, bf16[384,128]{1,0:T(8,128)(2,1)}, u32[]{:S(2)}) copy-start(bf16[384,128]{1,0:T(8,128)(2,1)} %first_ref.3) | copy-start | bytes 294916
  1.3 0.8 %copy-start.3 = (bf16[256,128]{1,0:T(8,128)(2,1)S(1)}, bf16[256,128]{1,0:T(8,128)(2,1)}, u32[]{:S(2)}) copy-start(bf16[256,128]{1,0:T(8,128)(2,1)} %first_ref.2) | copy-start | bytes 196612
  2.2 0.8 %copy-start.5 = (bf16[128,128]{1,0:T(8,128)(2,1)S(1)}, bf16[128,128]{1,0:T(8,128)(2,1)}, u32[]{:S(2)}) copy-start(bf16[128,128]{1,0:T(8,128)(2,1)} %second_ref.2) | copy-start | bytes 98308
  2.9 0.7 %copy-start.8 = (bf16[64,128]{1,0:T(8,128)(2,1)S(1)}, bf16[64,128]{1,0:T(8,128)(2,1)}, u32[]{:S(2)}) copy-start(bf16[64,128]{1,0:T(8,128)(2,1)} %lat_ref.1) | copy-start | bytes 49156
  3.6 0.7 %copy-start.9 = (bf16[64,128]{1,0:T(8,128)(2,1)S(1)}, bf16[64,128]{1,0:T(8,128)(2,1)}, u32[]{:S(2)}) copy-start(bf16[64,128]{1,0:T(8,128)(2,1)} %sum_ref.1) | copy-start | bytes 49156
  4.4 0.7 %copy-start.10 = (bf16[64,128]{1,0:T(8,128)(2,1)S(1)}, bf16[64,128]{1,0:T(8,128)(2,1)}, u32[]{:S(2)}) copy-start(bf16[64,128]{1,0:T(8,128)(2,1)} %glo_ref.1) | copy-start | bytes 49156
  5.1 0.7 %copy-start.11 = (f32[128]{0:T(128)S(1)}, f32[128]{0:T(128)}, u32[]{:S(2)}) copy-start(f32[128]{0:T(128)} %param.31) | copy-start | bytes 1540
  5.7 12.1 %copy-start.4 = (bf16[128,128]{1,0:T(8,128)(2,1)S(1)}, bf16[128,128]{1,0:T(8,128)(2,1)}, u32[]{:S(2)}) copy-start(bf16[128,128]{1,0:T(8,128)(2,1)} %second_ref.3) | copy-start | bytes 98308
  5.7 12.1 %copy-start.6 = (s32[32,128]{1,0:T(8,128)S(1)}, s32[32,128]{1,0:T(8,128)}, u32[]{:S(2)}) copy-start(s32[32,128]{1,0:T(8,128)} %rslot_ref.1) | copy-start | bytes 49156
  5.7 12.2 %copy-start.7 = (s32[32,128]{1,0:T(8,128)S(1)}, s32[32,128]{1,0:T(8,128)}, u32[]{:S(2)}) copy-start(s32[32,128]{1,0:T(8,128)} %sslot_ref.1) | copy-start | bytes 49156
  17.8 0.7 %copy-start.12 = (s32[32]{0:T(128)S(1)}, s32[32]{0:T(128)}, u32[]{:S(2)}) copy-start(s32[32]{0:T(128)} %trecv_ref.1) | copy-start | bytes 388
  17.8 0.7 %copy-start.13 = (s32[32]{0:T(128)S(1)}, s32[32]{0:T(128)}, u32[]{:S(2)}) copy-start(s32[32]{0:T(128)} %tsend_ref.1) | copy-start | bytes 388
  17.8 0.7 %copy-start.14 = (f32[128]{0:T(128)S(1)}, f32[128]{0:T(128)}, u32[]{:S(2)}) copy-start(f32[128]{0:T(128)} %param.28) | copy-start | bytes 1540
  18.5 1.2 %copy-start = (bf16[32,128,128]{2,1,0:T(8,128)(2,1)S(1)}, bf16[32,128,128]{2,1,0:T(8,128)(2,1)}, u32[]{:S(2)}) copy-start(bf16[32,128,128]{2,1,0:T(8,128)(2,1)} %edge_ref.1) | copy-start | bytes 3145732
  19.7 1.2 %copy-start.1 = (bf16[32,128,128]{2,1,0:T(8,128)(2,1)S(1)}, bf16[32,128,128]{2,1,0:T(8,128)(2,1)}, u32[]{:S(2)}) copy-start(bf16[32,128,128]{2,1,0:T(8,128)(2,1)} %grad_ref.1) | copy-start | bytes 3145732

commit v2 on v1

--- a/solution.py
+++ b/solution.py
@@ -12,7 +12,8 @@
 F32 = jnp.float32
 BF16 = jnp.bfloat16
 GROUP = 8
-PAIR = 2
+PAIR = 8
+LIMIT = 56 << 20
 
 
 def dot(a, b):
@@ -38,44 +39,58 @@
 
 
 def node_kernel(
-    nr, nc, lat_ref, sum_ref, glo_ref, first_ref, second_ref, gain_ref,
+    nr, nc, lat_hbm, sum_hbm, glo_hbm, first_hbm, second_hbm, gain_hbm,
     rlat_ref, rgrad_ref, slat_ref, base_ref, wn_ref,
-    gs_buf, lat_send, lat_recv, gs_send, gs_recv, sl_send, sl_recv,
+    lat_ref, sum_ref, glo_ref, first_ref, second_ref, gain_ref, gs_buf, in_sems,
+    lat_send, lat_recv, lf_send, lf_recv, gs_send, gs_recv, gf_send, gf_recv,
+    sl_send, sl_recv, sf_send, sf_recv,
 ):
     row, col, rep = lax.axis_index("row"), lax.axis_index("col"), lax.axis_index("rep")
     rows, width = lat_ref.shape
-    nrr, ncr = nr * 2, nc * 2
-    mine_r, mine_c = row * 2 + rep, col * 2 + rep
+    twin = {"rep": 1 - rep}
+    loads = []
+    for i, (src, dst) in enumerate((
+        (lat_hbm, lat_ref), (sum_hbm, sum_ref), (first_hbm, first_ref),
+        (second_hbm, second_ref), (glo_hbm, glo_ref), (gain_hbm, gain_ref),
+    )):
+        loads.append(pltpu.make_async_copy(src, dst, in_sems.at[i]))
+        loads[-1].start()
 
     def r_dev(k):
-        other = lax.rem(mine_r + k, nrr)
-        return {"row": lax.div(other, 2), "rep": lax.rem(other, 2)}
+        return {"row": lax.rem(row + k, nr)}
 
     def c_dev(k):
-        other = lax.rem(mine_c + k, ncr)
-        return {"col": lax.div(other, 2), "rep": lax.rem(other, 2)}
+        return {"col": lax.rem(col + k, nc)}
 
     barrier = pltpu.get_barrier_semaphore()
-    for k in range(1, nrr):
+    pl.semaphore_signal(barrier, inc=1, device_id=twin, device_id_type=MESH)
+    for k in range(1, nr):
         pl.semaphore_signal(barrier, inc=1, device_id=r_dev(k), device_id_type=MESH)
-    for k in range(1, ncr):
+    for k in range(1, nc):
         pl.semaphore_signal(barrier, inc=1, device_id=c_dev(k), device_id_type=MESH)
-    pl.semaphore_wait(barrier, nrr + ncr - 2)
-
-    r_here = pl.ds(pl.multiple_of(mine_r * rows, 16), rows)
-    c_here = pl.ds(pl.multiple_of(mine_c * rows, 16), rows)
-    lat_copies, sl_copies, gs_copies = [], [], []
-    for k in range(1, nrr):
-        lat_copies.append(pltpu.make_async_remote_copy(
-            src_ref=lat_ref, dst_ref=rlat_ref.at[r_here], send_sem=lat_send.at[k],
-            recv_sem=lat_recv.at[k], device_id=r_dev(k), device_id_type=MESH))
-        lat_copies[-1].start()
-    for k in range(1, ncr):
-        sl_copies.append(pltpu.make_async_remote_copy(
-            src_ref=lat_ref, dst_ref=slat_ref.at[c_here], send_sem=sl_send.at[k],
-            recv_sem=sl_recv.at[k], device_id=c_dev(k), device_id_type=MESH))
-        sl_copies[-1].start()
-
+    loads[0].wait()
+    pl.semaphore_wait(barrier, nr + nc - 1)
+
+    def send(src, dst, send_sem, recv_sem, device):
+        copy = pltpu.make_async_remote_copy(
+            src_ref=src, dst_ref=dst, send_sem=send_sem, recv_sem=recv_sem,
+            device_id=device, device_id_type=MESH)
+        copy.start()
+        return copy
+
+    def at(index):
+        return pl.ds(pl.multiple_of(index * rows, 16), rows)
+
+    r_here, c_here = at(row * 2 + rep), at(col * 2 + rep)
+    lats = [send(lat_ref, rlat_ref.at[r_here], lat_send.at[k], lat_recv.at[k], r_dev(k))
+            for k in range(1, nr)]
+    slats = [send(lat_ref, slat_ref.at[c_here], sl_send.at[k], sl_recv.at[k], c_dev(k))
+             for k in range(1, nc)]
+    passed = [send(lat_ref, rlat_ref.at[r_here], lf_send.at[0], lf_recv.at[0], twin),
+              send(lat_ref, slat_ref.at[c_here], sf_send.at[0], sf_recv.at[0], twin)]
+
+    for load in loads[1:]:
+        load.wait()
     lat = lat_ref[...]
     inputs = jnp.concatenate([lat, sum_ref[...]], axis=1)
     pre = dot(inputs, first_ref[...])
@@ -85,27 +100,36 @@
     grad_raw, gain_term = norm_back(raw, upstream, gain_ref[...])
     grad_hidden = dot_nt(grad_raw, second_ref[...])
     grad_pre = jnp.where(pre > 0.0, grad_hidden, 0.0).astype(BF16)
-    grad_in = dot_nt(grad_pre, first_ref[...])
-    grad_sum = grad_in[:, width:].astype(BF16)
+    grad_sum = dot_nt(grad_pre, first_ref[width:, :]).astype(BF16)
     gs_buf[...] = grad_sum
-    for k in range(1, nrr):
-        gs_copies.append(pltpu.make_async_remote_copy(
-            src_ref=gs_buf, dst_ref=rgrad_ref.at[r_here], send_sem=gs_send.at[k],
-            recv_sem=gs_recv.at[k], device_id=r_dev(k), device_id_type=MESH))
-        gs_copies[-1].start()
+    grads = [send(gs_buf, rgrad_ref.at[r_here], gs_send.at[k], gs_recv.at[k], r_dev(k))
+             for k in range(1, nr)]
+    passed.append(send(gs_buf, rgrad_ref.at[r_here], gf_send.at[0], gf_recv.at[0], twin))
+    for k in range(1, nr):
+        lats[k - 1].wait_recv()
+        block = rlat_ref.at[at(lax.rem(row + nr - k, nr) * 2 + rep)]
+        passed.append(send(block, block, lf_send.at[k], lf_recv.at[k], twin))
+    for k in range(1, nc):
+        slats[k - 1].wait_recv()
+        block = slat_ref.at[at(lax.rem(col + nc - k, nc) * 2 + rep)]
+        passed.append(send(block, block, sf_send.at[k], sf_recv.at[k], twin))
     rlat_ref[r_here, :] = lat
     rgrad_ref[r_here, :] = grad_sum
     slat_ref[c_here, :] = lat
-    base_ref[...] = upstream + grad_in[:, :width]
+    base_ref[...] = upstream + dot_nt(grad_pre, first_ref[0:width, :])
     w1 = first_ref.shape[0]
     w2 = w1 + second_ref.shape[0]
     wn_ref[0:w1, :] = dot(inputs.T, grad_pre).astype(BF16)
     wn_ref[w1:w2, :] = dot(hidden.T, grad_raw).astype(BF16)
     wn_ref[w2:w2 + 16, :] = jnp.broadcast_to(
         jnp.sum(gain_term, axis=0, keepdims=True), (16, width)).astype(BF16)
-    for copy in lat_copies + sl_copies + gs_copies:
+    for k in range(1, nr):
+        grads[k - 1].wait_recv()
+        block = rgrad_ref.at[at(lax.rem(row + nr - k, nr) * 2 + rep)]
+        passed.append(send(block, block, gf_send.at[k], gf_recv.at[k], twin))
+    for copy in passed:
         copy.wait_recv()
-    for copy in lat_copies + sl_copies + gs_copies:
+    for copy in lats + slats + grads + passed:
         copy.wait_send()
 
 
@@ -225,8 +249,8 @@
 
 def sum_kernel(
     nr, nc, chunk, pack_ref, base_ref,
-    glat_ref, ef_ref, es_ref, eg_ref, nf_ref, ns_ref, ng_ref,
-    buf, part, rbuf, sbuf, wbuf, wfin,
+    glat_ref, wfin,
+    buf, part, rbuf, sbuf, wbuf,
     p_send, p_recv, w_send, w_recv, r_send, r_recv, s_send, s_recv,
     a_send, a_recv, f_send, f_recv,
 ):
@@ -311,17 +335,37 @@
         f_copies.append(send(passed, passed, f_send.at[k], f_recv.at[k], twin))
     for copy in f_copies:
         copy.wait_recv()
+    for copy in [p_w, p_n] + w_copies + r_copies + s_copies + a_copies + f_copies:
+        copy.wait_send()
+
+
+def write_kernel(
+    glat_ref, wfin, glat_out, ef_out, es_out, eg_out, nf_out, ns_out, ng_out,
+    ef_ref, es_ref, eg_ref, nf_ref, ns_ref, ng_ref, sems,
+):
+    def store(i, src, dst):
+        copy = pltpu.make_async_copy(src, dst, sems.at[i])
+        copy.start()
+        return copy
+
+    copies = [store(0, glat_ref, glat_out)]
     nef, nes = ef_ref.shape[0], es_ref.shape[0]
     ef_ref[...] = wfin[0, 0:nef, :].astype(F32)
+    copies.append(store(1, ef_ref, ef_out))
     es_ref[...] = wfin[0, nef:nef + nes, :].astype(F32)
+    copies.append(store(2, es_ref, es_out))
     nnf, nns = nf_ref.shape[0], ns_ref.shape[0]
     nf_ref[...] = wfin[1, 0:nnf, :].astype(F32)
+    copies.append(store(3, nf_ref, nf_out))
     ns_ref[...] = wfin[1, nnf:nnf + nns, :].astype(F32)
+    copies.append(store(4, ns_ref, ns_out))
     gains = wfin[1, nnf + nns:nnf + nns + 32, :].astype(F32)
     ng_ref[...] = gains[0:1]
     eg_ref[...] = gains[16:17]
-    for copy in [p_w, p_n] + w_copies + r_copies + s_copies + a_copies + f_copies:
-        copy.wait_send()
+    copies.append(store(5, ng_ref, ng_out))
+    copies.append(store(6, eg_ref, eg_out))
+    for copy in copies:
+        copy.wait()
 
 
 def per_device(
@@ -335,27 +379,31 @@
     block = rows * 2
     chips = nr * nc
     vmem = pl.BlockSpec(memory_space=pltpu.VMEM)
+    hbm = pl.BlockSpec(memory_space=pl.ANY)
     dma = pltpu.SemaphoreType.DMA
     weight_rows = edge_first.shape[0] + edge_second.shape[0]
     node_rows = node_first.shape[0] + node_second.shape[0]
     chunk = -(-max(weight_rows, node_rows + 32) // (16 * chips)) * 16
     half_rows = chunk * chips
-    nrr, ncr = nr * 2, nc * 2
     shape = jax.ShapeDtypeStruct
 
     rlat, rgrad, slat, base, wn = pl.pallas_call(
         functools.partial(node_kernel, nr, nc),
         out_shape=(
-            shape((nrr * rows, width), BF16), shape((nrr * rows, width), BF16),
-            shape((ncr * rows, width), BF16), shape((rows, width), F32),
+            shape((nr * block, width), BF16), shape((nr * block, width), BF16),
+            shape((nc * block, width), BF16), shape((rows, width), F32),
             shape((node_rows + 16, width), BF16),
         ),
-        in_specs=[vmem] * 6,
+        in_specs=[hbm] * 6,
         out_specs=(vmem,) * 5,
-        scratch_shapes=[pltpu.VMEM((rows, width), BF16),
-                        dma((nrr,)), dma((nrr,)), dma((nrr,)), dma((nrr,)), dma((ncr,)), dma((ncr,))],
+        scratch_shapes=[
+            pltpu.VMEM((rows, width), BF16), pltpu.VMEM((rows, width), BF16),
+            pltpu.VMEM((rows, width), BF16), pltpu.VMEM(node_first.shape, BF16),
+            pltpu.VMEM(node_second.shape, BF16), pltpu.VMEM((1, width), F32),
+            pltpu.VMEM((rows, width), BF16), dma((6,)),
+        ] + [dma((nr,))] * 8 + [dma((nc,))] * 4,
         compiler_params=pltpu.CompilerParams(
-            collective_id=0, has_side_effects=True, vmem_limit_bytes=32 << 20),
+            collective_id=0, has_side_effects=True, vmem_limit_bytes=LIMIT),
     )(latents, saved_sum, grad_latents_out, node_first, node_second, node_gain.reshape(1, -1))
 
     def whole(*dims):
@@ -389,32 +437,40 @@
             ],
         ),
         compiler_params=pltpu.CompilerParams(
-            dimension_semantics=("arbitrary",), vmem_limit_bytes=40 << 20),
+            dimension_semantics=("arbitrary",), vmem_limit_bytes=LIMIT),
     )(
         tile_recv, tile_send, tile_count, edge_latents, grad_edges_out, recv_slot, send_slot,
         rlat.reshape(nr, block, width), rgrad.reshape(nr, block, width),
         slat.reshape(nc, block, width), edge_first, edge_second, edge_gain.reshape(1, -1), wn,
     )
 
-    outs = pl.pallas_call(
+    glat, totals = pl.pallas_call(
         functools.partial(sum_kernel, nr, nc, chunk),
-        out_shape=(
-            shape((rows, width), BF16), shape(edge_first.shape, F32),
-            shape(edge_second.shape, F32), shape((1, width), F32),
-            shape(node_first.shape, F32), shape(node_second.shape, F32), shape((1, width), F32),
-        ),
+        out_shape=(shape((rows, width), BF16), shape((2, half_rows, width), BF16)),
         in_specs=[vmem] * 2,
-        out_specs=(vmem,) * 7,
+        out_specs=(vmem,) * 2,
         scratch_shapes=[
             pltpu.VMEM((pack_rows, width), BF16), pltpu.VMEM((pack_rows, width), BF16),
             pltpu.VMEM((nr, rows, width), BF16), pltpu.VMEM((nc, rows, width), BF16),
-            pltpu.VMEM((chips, chunk, width), BF16), pltpu.VMEM((2, half_rows, width), BF16),
+            pltpu.VMEM((chips, chunk, width), BF16),
             dma((2,)), dma((2,)), dma((chips,)), dma((chips,)), dma((nr,)), dma((nr,)),
             dma((nc,)), dma((nc,)), dma((chips,)), dma((chips,)), dma((chips,)), dma((chips,)),
         ],
         compiler_params=pltpu.CompilerParams(
-            collective_id=1, has_side_effects=True, vmem_limit_bytes=40 << 20),
+            collective_id=1, has_side_effects=True, vmem_limit_bytes=LIMIT),
     )(pack, base)
+    finals = (
+        shape(edge_first.shape, F32), shape(edge_second.shape, F32), shape((1, width), F32),
+        shape(node_first.shape, F32), shape(node_second.shape, F32), shape((1, width), F32),
+    )
+    outs = pl.pallas_call(
+        write_kernel,
+        out_shape=(shape((rows, width), BF16),) + finals,
+        in_specs=[vmem] * 2,
+        out_specs=(hbm,) * 7,
+        scratch_shapes=[pltpu.VMEM(item.shape, F32) for item in finals] + [dma((7,))],
+        compiler_params=pltpu.CompilerParams(vmem_limit_bytes=LIMIT),
+    )(glat, totals)
     grad_latents, ef, es, eg, nf, ns, ng = outs
     return (grad_latents, grads_out, ef, es, eg.reshape(-1), nf, ns, ng.reshape(-1))
 

time: 59 us -> 42.5 us (0.72)
  local copies, waits for them, and re-layouts: 11.7 us -> 0 us
  Pallas kernels: 44.8 us -> 40.5 us
    unnamed x37 -> x0, local copies, waits for them, and re-layouts: 11.7 us -> none
    pallas_call x1, Pallas kernels: 17.5 us -> 11.6 us  [per_device(): pl.pallas_call(functools.partial(edge_kernel, nr, nc, half_rows), out_sha...]
    pallas_call x0 -> x1, Pallas kernels: none -> 1.81 us  [per_device(): pl.pallas_call(write_kernel, out_shape=(shape((rows, width), BF16),) + fi...]
    pallas_call x1, Pallas kernels: 12.1 us -> 11.2 us  [per_device(): pl.pallas_call(functools.partial(node_kernel, nr, nc), out_shape=(shape((...]
    pallas_call x1, Pallas kernels: 15.2 us -> 16 us  [per_device(): pl.pallas_call(functools.partial(sum_kernel, nr, nc, chunk), out_shape=(s...]
where the time goes in v2:
time: 42.5 us; the launch traced here: 41.8 us
  Pallas kernels  40.5 us (95%)
  between operations  1.3 us (3%)
    pallas_call x1, Pallas kernels, per_device(): pl.pallas_call(functools.partial(sum_kernel, nr, nc, chunk), out_shape=(s...  16 us
    pallas_call x1, Pallas kernels, per_device(): pl.pallas_call(functools.partial(edge_kernel, nr, nc, half_rows), out_sha...  11.6 us
    pallas_call x1, Pallas kernels, per_device(): pl.pallas_call(functools.partial(node_kernel, nr, nc), out_shape=(shape((...  11.2 us
    pallas_call x1, Pallas kernels, per_device(): pl.pallas_call(write_kernel, out_shape=(shape((rows, width), BF16),) + fi...  1.81 us

profile of v2, /device:TPU:0, one launch (start us, length us, event | category | flops | bytes accessed | tf_op | source)
XLA Modules:
  0.0 41.8 jit_solution(17400381812345017409)
XLA Ops:
  1.3 11.2 %shard_map.215 = (bf16[512,128]{1,0:T(8,128)(2,1)}, bf16[512,128]{1,0:T(8,128)(2,1)}, bf16[256,128]{1,0:T(8,128)(2,1)}, f32[64,128]{1,0:T(8,128)}, bf16[400,128]{1,0:T(8,128)(2,1)}) custom-call(bf16[64,128]{1,0:T(8,128)(2,1)} %lat_hbm.1, bf16[64,128]{1,0:T(8,128)(2,1)} %sum_hbm.1, bf16[64,128]{1,0:T(8,128)(2,1)} %glo_hbm.1, bf16[256,128]{1,0:T(8,128)(2,1)} %first_hbm.1, ...), custom_call_target="tpu_custom_call" | custom-call | tf_op jit(solution)/shard_map/pallas_call | solution.py:390
  12.5 11.6 %shard_map.216 = (bf16[32,128,128]{2,1,0:T(8,128)(2,1)}, bf16[2,896,128]{2,1,0:T(8,128)(2,1)}) custom-call(s32[32]{0:T(128)} %trecv_ref.1, s32[32]{0:T(128)} %tsend_ref.1, s32[1]{0:T(128)S(6)} %copy.24.count_ref, bf16[32,128,128]{2,1,0:T(8,128)(2,1)} %edge_ref.1, bf16[32,128,128]{2,1,0:T(8,128)(2,1)} %grad_ref.1, s32[32,128]{1,0:T(8,128)} %rslot_ref.1, ...), custom_call_target="tpu_custom_call" | custom-call | tf_op jit(solution)/shard_map/pallas_call | solution.py:415
  24.0 16.0 %shard_map.217 = (bf16[64,128]{1,0:T(8,128)(2,1)}, bf16[2,512,128]{2,1,0:T(8,128)(2,1)}) custom-call(bf16[2,896,128]{2,1,0:T(8,128)(2,1)} %get-tuple-element.28.pack_ref, f32[64,128]{1,0:T(8,128)} %get-tuple-element.29.base_ref), custom_call_target="tpu_custom_call" | custom-call | tf_op jit(solution)/shard_map/pallas_call | solution.py:447
  40.0 1.8 %shard_map.218 = (bf16[64,128]{1,0:T(8,128)(2,1)}, f32[384,128]{1,0:T(8,128)}, f32[128,128]{1,0:T(8,128)}, f32[1,128]{1,0:T(1,128)}, f32[256,128]{1,0:T(8,128)}, /*index=5*/f32[128,128]{1,0:T(8,128)}, f32[1,128]{1,0:T(1,128)}) custom-call(bf16[64,128]{1,0:T(8,128)(2,1)} %get-tuple-element.30.glat_ref, bf16[2,512,128]{2,1,0:T(8,128)(2,1)} %get-tuple-element.31.wfin), custom_call_target="tpu_custom_call" | custom-call | tf_op jit(solution)/shard_map/pallas_call | solution.py:466

commit v3 on v2

--- a/solution.py
+++ b/solution.py
@@ -11,7 +11,7 @@
 MESH = pl.DeviceIdType.MESH
 F32 = jnp.float32
 BF16 = jnp.bfloat16
-GROUP = 8
+GROUP = 16
 PAIR = 8
 LIMIT = 56 << 20
 
@@ -457,7 +457,7 @@
             dma((nc,)), dma((nc,)), dma((chips,)), dma((chips,)), dma((chips,)), dma((chips,)),
         ],
         compiler_params=pltpu.CompilerParams(
-            collective_id=1, has_side_effects=True, vmem_limit_bytes=LIMIT),
+            collective_id=1, has_side_effects=True, vmem_limit_bytes=24 << 20),
     )(pack, base)
     finals = (
         shape(edge_first.shape, F32), shape(edge_second.shape, F32), shape((1, width), F32),
@@ -469,7 +469,7 @@
         in_specs=[vmem] * 2,
         out_specs=(hbm,) * 7,
         scratch_shapes=[pltpu.VMEM(item.shape, F32) for item in finals] + [dma((7,))],
-        compiler_params=pltpu.CompilerParams(vmem_limit_bytes=LIMIT),
+        compiler_params=pltpu.CompilerParams(vmem_limit_bytes=24 << 20),
     )(glat, totals)
     grad_latents, ef, es, eg, nf, ns, ng = outs
     return (grad_latents, grads_out, ef, es, eg.reshape(-1), nf, ns, ng.reshape(-1))

time: 42.5 us -> 39.7 us (0.934); the launches traced: 41.8 us -> 40 us
  Pallas kernels: 40.5 us -> 37.7 us
  local copies, waits for them, and re-layouts: 0 us -> 1.02 us
    pallas_call x1, Pallas kernels: 11.6 us -> 10.5 us  [per_device(): pl.pallas_call(functools.partial(edge_kernel, nr, nc, half_rows), out_sha...]
    unnamed x0 -> x4, local copies, waits for them, and re-layouts: none -> 1.02 us
    pallas_call x1, Pallas kernels: 1.81 us -> 0.84 us  [per_device(): pl.pallas_call(write_kernel, out_shape=(shape((rows, width), BF16),) + fi...]
    pallas_call x1, Pallas kernels: 16 us -> 15.2 us  [per_device(): pl.pallas_call(functools.partial(sum_kernel, nr, nc, chunk), out_shape=(s...]
where the time goes in v3:
time: 39.7 us; the launch traced here: 40 us
  Pallas kernels  37.7 us (95%)
  between operations  1.32 us (3%)
  local copies, waits for them, and re-layouts  1.02 us (3%)
    pallas_call x1, Pallas kernels, per_device(): pl.pallas_call(functools.partial(sum_kernel, nr, nc, chunk), out_shape=(s...  15.2 us
    pallas_call x1, Pallas kernels, per_device(): pl.pallas_call(functools.partial(node_kernel, nr, nc), out_shape=(shape((...  11.2 us
    pallas_call x1, Pallas kernels, per_device(): pl.pallas_call(functools.partial(edge_kernel, nr, nc, half_rows), out_sha...  10.5 us
    unnamed x4, local copies, waits for them, and re-layouts  1.02 us
    pallas_call x1, Pallas kernels, per_device(): pl.pallas_call(write_kernel, out_shape=(shape((rows, width), BF16),) + fi...  0.84 us

profile of v3, /device:TPU:0, one launch (start us, length us, event | category | flops | bytes accessed | tf_op | source)
XLA Modules:
  0.0 40.0 jit_solution(10519354671378343217)
XLA Ops:
  1.3 11.2 %shard_map.215 = (bf16[512,128]{1,0:T(8,128)(2,1)}, bf16[512,128]{1,0:T(8,128)(2,1)}, bf16[256,128]{1,0:T(8,128)(2,1)}, f32[64,128]{1,0:T(8,128)}, bf16[400,128]{1,0:T(8,128)(2,1)}) custom-call(bf16[64,128]{1,0:T(8,128)(2,1)} %lat_hbm.1, bf16[64,128]{1,0:T(8,128)(2,1)} %sum_hbm.1, bf16[64,128]{1,0:T(8,128)(2,1)} %glo_hbm.1, bf16[256,128]{1,0:T(8,128)(2,1)} %first_hbm.1, ...), custom_call_target="tpu_custom_call" | custom-call | tf_op jit(solution)/shard_map/pallas_call | solution.py:390
  12.5 0.0 copy-start.1
  12.5 10.5 %shard_map.216 = (bf16[32,128,128]{2,1,0:T(8,128)(2,1)}, bf16[2,896,128]{2,1,0:T(8,128)(2,1)}) custom-call(s32[32]{0:T(128)} %trecv_ref.1, s32[32]{0:T(128)} %tsend_ref.1, s32[1]{0:T(128)S(6)} %copy.24.count_ref, bf16[32,128,128]{2,1,0:T(8,128)(2,1)} %edge_ref.1, bf16[32,128,128]{2,1,0:T(8,128)(2,1)} %grad_ref.1, s32[32,128]{1,0:T(8,128)} %rslot_ref.1, ...), custom_call_target="tpu_custom_call" | custom-call | tf_op jit(solution)/shard_map/pallas_call | solution.py:415
  23.0 0.0 copy-done.1
  23.0 0.0 copy-start
  23.0 1.0 %copy-done = bf16[2,896,128]{2,1,0:T(8,128)(2,1)S(1)} copy-done((bf16[2,896,128]{2,1,0:T(8,128)(2,1)S(1)}, bf16[2,896,128]{2,1,0:T(8,128)(2,1)}, u32[]{:S(2)}) %copy-start) | copy-done | bytes 458776
  24.0 15.2 %shard_map.217 = (bf16[64,128]{1,0:T(8,128)(2,1)S(1)}, bf16[2,512,128]{2,1,0:T(8,128)(2,1)S(1)}) custom-call(bf16[2,896,128]{2,1,0:T(8,128)(2,1)S(1)} %copy-done, f32[64,128]{1,0:T(8,128)S(1)} %copy-done.1), custom_call_target="tpu_custom_call" | custom-call | tf_op jit(solution)/shard_map/pallas_call | solution.py:447
  39.2 0.8 %shard_map.218 = (bf16[64,128]{1,0:T(8,128)(2,1)}, f32[384,128]{1,0:T(8,128)}, f32[128,128]{1,0:T(8,128)}, f32[1,128]{1,0:T(1,128)}, f32[256,128]{1,0:T(8,128)}, /*index=5*/f32[128,128]{1,0:T(8,128)}, f32[1,128]{1,0:T(1,128)}) custom-call(bf16[64,128]{1,0:T(8,128)(2,1)S(1)} %get-tuple-element.30.glat_ref, bf16[2,512,128]{2,1,0:T(8,128)(2,1)S(1)} %get-tuple-element.31.wfin), custom_call_target="tpu_custom_call" | custom-call | tf_op jit(solution)/shard_map/pallas_call | solution.py:466
Async XLA Ops:
  12.5 10.5 %copy-start.1 = (f32[64,128]{1,0:T(8,128)S(1)}, f32[64,128]{1,0:T(8,128)}, u32[]{:S(2)}) copy-start(f32[64,128]{1,0:T(8,128)} %get-tuple-element.29.base_ref) | copy-start | bytes 98308
  23.0 1.0 %copy-start = (bf16[2,896,128]{2,1,0:T(8,128)(2,1)S(1)}, bf16[2,896,128]{2,1,0:T(8,128)(2,1)}, u32[]{:S(2)}) copy-start(bf16[2,896,128]{2,1,0:T(8,128)(2,1)} %get-tuple-element.28.pack_ref) | copy-start | bytes 1376260
